TPU v7x, 256 devices: a whole 4x4x8 slice. The times are simulated.
256 devices in a mesh: src: 16 (over z, x_hi), dom: 16 (over y, x_lo, core).
Axes of the slice: x: 4 (x_hi: 2, x_lo: 2; x = x_hi * 2 + x_lo), y: 4, z: 8, core: 2. Of those that a mesh axis runs over, the one named last changes fastest.
Arguments:
- primary: float32 [16, 4, 32, 128, 128], P('src', None, 'dom'), may hold values from -6 to 6
- conductivity: float32 [3, 32, 128, 128], P(None, 'dom'), may hold values from 0.5 to 2
- observed: float32 [16, 4, 1024], P('src'), may hold values from -6 to 6
- receivers: int32 [16, 1024], P('src'), may hold values from 0 to 524287
Outputs:
- gradient: float32 [3, 32, 128, 128], P(None, 'dom')
- predicted: float32 [16, 4, 1024], P('src')
Inputs may be any that keep to these rules, and one draw needn't show every extreme that they name: receivers may share a cell.
All inputs are finite; a program needn't handle non-finite values.
Results may differ from a plain program's by a relative error of at most 0.0001.
Values sent between devices are 32-bit elements; how exact they have to be, the bound alone decides.
No kernel may reach another device: no remote copies, remote signals or barrier semaphores. Data moves between devices by JAX's collectives and lax.ppermute only.
A program may use at most 128 MiB of HBM per device.

v0:
```python
import jax
import jax.numpy as jnp
from jax import lax
from jax.sharding import PartitionSpec as P

ITERS = 3


def extended_2(block, sides, width):
    for axis, dim in sides:
        count = lax.axis_size(axis)
        forward = [(i, i + 1) for i in range(count - 1)]
        backward = [(target, source) for source, target in forward]
        low = lax.ppermute(
            lax.slice_in_dim(block, block.shape[dim] - width, None, axis=dim), axis, forward
        )
        high = lax.ppermute(lax.slice_in_dim(block, 0, width, axis=dim), axis, backward)
        block = jnp.concatenate([low, block, high], axis=dim)
    return block


def neighbour_upper(field, along):
    extent = field.shape[along]
    inner_part = lax.slice_in_dim(field, 1, extent, axis=along)
    zeros_part = jnp.zeros_like(lax.slice_in_dim(field, 0, 1, axis=along))
    return jnp.concatenate([inner_part, zeros_part], axis=along)


def neighbour_lower(field, along):
    extent = field.shape[along]
    inner_part = lax.slice_in_dim(field, 0, extent - 1, axis=along)
    zeros_part = jnp.zeros_like(lax.slice_in_dim(field, 0, 1, axis=along))
    return jnp.concatenate([zeros_part, inner_part], axis=along)


def face_pair(conduct, along):
    return (
        0.5 * (conduct + neighbour_upper(conduct, along)),
        0.5 * (conduct + neighbour_lower(conduct, along)),
    )


def diagonal_of(face_list):
    result = face_list[0][0] + face_list[0][1]
    for component in (1, 2):
        result = result + face_list[component][0] + face_list[component][1]
    return result


def operate(extended, face_list, diagonal):
    field = extended[:, 1:-1]
    result = diagonal * field
    upper, lower = face_list[0]
    result = result - upper * extended[:, 2:] - lower * extended[:, :-2]
    for component in (1, 2):
        upper, lower = face_list[component]
        result = (
            result
            - upper * neighbour_upper(field, component + 1)
            - lower * neighbour_lower(field, component + 1)
        )
    return result


def column(values):
    return values[:, None, None, None]


def local_inner(left, right):
    return jnp.sum(left * right, axis=(1, 2, 3))


def extend_rims(field):
    return extended_2(field, (("dom", 1),), 1)


def summed(values):
    return lax.psum(values, "dom")


def precond_solve(right_side, face_list, diagonal):
    iterate = jnp.zeros_like(right_side)
    rim_low = jnp.zeros_like(right_side[:, :1])
    rim_high = jnp.zeros_like(right_side[:, :1])
    residual = right_side
    scaled = residual / diagonal
    direction = scaled
    norm_now = summed(local_inner(residual, scaled))
    for iteration in range(ITERS):
        dir_ext = extend_rims(direction)
        image = operate(dir_ext, face_list, diagonal)
        step_len = column(norm_now / summed(local_inner(direction, image)))
        iterate = iterate + step_len * direction
        rim_low = rim_low + step_len * dir_ext[:, :1]
        rim_high = rim_high + step_len * dir_ext[:, -1:]
        residual = residual - step_len * image
        if iteration + 1 < ITERS:
            scaled = residual / diagonal
            norm_next = summed(local_inner(residual, scaled))
            direction = scaled + column(norm_next / norm_now) * direction
            norm_now = norm_next
    return (iterate, rim_low, rim_high)


def per_device(primary, conductivity, observed, receivers):
    primary_g = primary[0]
    observed_g = observed[0]
    cells_g = receivers[0]
    domains = lax.axis_size("dom")
    position = lax.axis_index("dom")
    sources, layers, extent_y, extent_z = primary_g.shape
    stacked = jnp.concatenate([primary_g, conductivity[0:1]], axis=0)
    extended = extended_2(stacked, (("dom", 1),), 1)
    primary_ext = extended[:sources]
    cond_ext = extended[sources]
    cond_first = conductivity[0]
    face_list = [(0.5 * (cond_first + cond_ext[2:]), 0.5 * (cond_first + cond_ext[:-2]))]
    face_list = face_list + [face_pair(conductivity[component], component) for component in (1, 2)]
    diagonal = diagonal_of(face_list)
    layer_pos = lax.broadcasted_iota(jnp.int32, (layers, extent_y, extent_z), 0)
    at_top = jnp.logical_and(position == domains - 1, layer_pos == layers - 1)
    at_bottom = jnp.logical_and(position == 0, layer_pos == 0)
    ones_field = jnp.ones((layers, extent_y, extent_z), jnp.float32)
    unit_faces = [
        (
            jnp.where(at_top, 0.5, 1.0).astype(jnp.float32),
            jnp.where(at_bottom, 0.5, 1.0).astype(jnp.float32),
        )
    ]
    unit_faces = unit_faces + [face_pair(ones_field, component) for component in (1, 2)]
    unit_diagonal = diagonal_of(unit_faces)
    right_side = operate(primary_ext, unit_faces, unit_diagonal) - operate(
        primary_ext, face_list, diagonal
    )
    secondary, sec_low, sec_high = precond_solve(right_side, face_list, diagonal)
    potential = primary_g + secondary
    pot_ext = jnp.concatenate(
        [primary_ext[:, :1] + sec_low, potential, primary_ext[:, -1:] + sec_high], axis=1
    )
    plane_size = extent_y * extent_z
    layer_of = cells_g // plane_size
    in_plane = cells_g - layer_of * plane_size
    local_layer = layer_of - position * layers
    inside = jnp.logical_and(local_layer >= 0, local_layer < layers)
    local_cell = jnp.clip(local_layer, 0, layers - 1) * plane_size + in_plane
    flattened = potential.reshape(sources, -1)
    picked = jnp.where(inside[None, :], jnp.take(flattened, local_cell, axis=1), 0.0)
    predicted = lax.psum(picked, "dom")
    weights = jnp.where(inside[None, :], predicted - observed_g, 0.0)
    source = jnp.zeros_like(flattened).at[:, local_cell].add(weights).reshape(potential.shape)
    adjoint, adj_low, adj_high = precond_solve(source, face_list, diagonal)
    adj_ext = jnp.concatenate([adj_low, adjoint, adj_high], axis=1)
    upper_term = (potential - pot_ext[:, 2:]) * (adjoint - adj_ext[:, 2:])
    lower_term = (potential - pot_ext[:, :-2]) * (adjoint - adj_ext[:, :-2])
    pieces = [-0.5 * jnp.sum(upper_term + lower_term, axis=0)]
    for component in (1, 2):
        along = component + 1
        upper_term = (potential - neighbour_upper(potential, along)) * (
            adjoint - neighbour_upper(adjoint, along)
        )
        lower_term = (potential - neighbour_lower(potential, along)) * (
            adjoint - neighbour_lower(adjoint, along)
        )
        pieces.append(-0.5 * jnp.sum(upper_term + lower_term, axis=0))
    local_grad = jnp.stack(pieces)
    summed_grad = lax.psum(local_grad, "src")
    return (summed_grad, predicted[None])


def solution(mesh):
    placed = (
        P("src", None, "dom", None, None),
        P(None, "dom", None, None),
        P("src", None, None),
        P("src", None),
    )
    return jax.shard_map(
        per_device,
        mesh=mesh,
        in_specs=placed,
        out_specs=(P(None, "dom", None, None), P("src", None, None)),
        check_vma=False,
    )
```

profile of v0, /device:TPU:8, one launch (start us, length us, event | category | flops | bytes accessed | tf_op | source)
XLA Modules:
  0.0 665.1 jit_solution(13524334445278450123)
XLA Ops:
  11.3 4.5 collective-permute-start
  34.7 4.1 collective-permute-done.3
  39.5 22.3 %all-reduce.41 = (f32[4]{0:T(128)S(1)}, f32[4]{0:T(128)S(1)}) all-reduce(f32[4]{0:T(128)S(1)} %get-tuple-element.10, f32[4]{0:T(128)S(1)} %get-tuple-element.9), channel_id=1, replica_groups=mesh['src'=16,'dom'=16] {'dom'}, use_global_device_ids=true, to_apply=%region_1.2 | all-reduce | flops 8 | bytes 64 | tf_op jit(solution)/shard_map/psum | solution.py:78
  62.1 24.5 %psum.100 = f32[4]{0:T(128)S(1)} all-reduce(f32[4]{0:T(128)S(1)} %get-tuple-element.23), channel_id=1, replica_groups=mesh['src'=16,'dom'=16] {'dom'}, use_global_device_ids=true, to_apply=%region_5.6 | all-reduce | flops 4 | bytes 32 | tf_op jit(solution)/shard_map/psum | solution.py:78
  86.9 5.1 collective-permute-start.4
  94.1 3.5 collective-permute-done.4
  97.6 5.6 collective-permute-done.5
  104.0 22.9 %psum.101 = f32[4]{0:T(128)} all-reduce(f32[4]{0:T(128)S(1)} %get-tuple-element.21), channel_id=1, replica_groups=mesh['src'=16,'dom'=16] {'dom'}, use_global_device_ids=true, to_apply=%region_7.8 | all-reduce | flops 4 | bytes 32 | tf_op jit(solution)/shard_map/psum | solution.py:78
  128.9 25.8 %psum.102 = f32[4]{0:T(128)} all-reduce(f32[4]{0:T(128)} %multiply_reduce_fusion.4), channel_id=1, replica_groups=mesh['src'=16,'dom'=16] {'dom'}, use_global_device_ids=true, to_apply=%region_9.10 | all-reduce | flops 4 | bytes 32 | tf_op jit(solution)/shard_map/psum | solution.py:78
  156.6 5.7 collective-permute-start.6
  164.5 3.5 collective-permute-done.6
  168.0 5.6 collective-permute-done.7
  176.7 22.3 %psum.103 = f32[4]{0:T(128)S(1)} all-reduce(f32[4]{0:T(128)S(1)} %fusion.64), channel_id=1, replica_groups=mesh['src'=16,'dom'=16] {'dom'}, use_global_device_ids=true, to_apply=%region_11.12 | all-reduce | flops 4 | bytes 32 | tf_op jit(solution)/shard_map/psum | solution.py:78
  200.5 8.6 %copy.11 = f32[4,2,128,128]{0,3,2,1:T(8,128)} copy(f32[4,2,128,128]{3,2,1,0:T(8,128)S(1)} %add_add_fusion) | data formatting | bytes 1048576 | tf_op jit(solution)/shard_map/add | solution.py:136
  209.1 8.6 %gather_fusion = f32[1024,4]{1,0:T(8,128)S(1)} fusion(f32[4,32768]{0,1:T(8,128)} %bitcast.78, s32[1024]{0:T(1024)S(1)} %broadcast_clamp_fusion), kind=kCustom, calls=%fused_computation | custom fusion | bytes 36864 | tf_op jit(solution)/shard_map/jit(_take)/gather | solution.py:147
  218.7 55.9 %psum.104 = f32[4,1024]{0,1:T(8,128)S(1)} all-reduce(f32[4,1024]{0,1:T(8,128)S(1)} %select_bitcast_fusion), channel_id=1, replica_groups=mesh['src'=16,'dom'=16] {'dom'}, use_global_device_ids=true, to_apply=%region_12.13 | all-reduce | flops 4096 | bytes 32768 | tf_op jit(solution)/shard_map/psum | solution.py:148
  274.6 13.4 %scatter_custom_fusion = f32[4,32768]{0,1:T(8,128)} fusion(s32[1024]{0:T(1024)S(1)} %bitcast.82, f32[]{:T(128)} %constant.79.clone.1, f32[4,1024]{0,1:T(8,128)S(1)} %psum.104, f32[1,4,1024]{1,2,0:T(8,128)S(1)} %copy-done.8, pred[1024]{0:T(1024)(128)(4,1)S(1)} %and_reduce_fusion), kind=kCustom, calls=%fused_computation.4 | custom fusion | flops 12288 | bytes 1574912 | tf_op jit(solution)/shard_map/scatter-add | solution.py:150
  288.0 10.1 %copy.13 = f32[4,2,128,128]{3,2,1,0:T(8,128)S(1)} copy(f32[4,2,128,128]{0,3,2,1:T(8,128)} %bitcast.71) | data formatting | bytes 1048576 | tf_op jit(solution)/shard_map/reshape | solution.py:150
  298.5 15.3 %fusion = f32[4]{0:T(128)S(1)} fusion(f32[4,32768]{0,1:T(8,128)} %scatter_custom_fusion, f32[32768]{0:T(1024)S(1)} %bitcast.72), kind=kLoop, calls=%fused_computation.3 | loop fusion | flops 393212 | bytes 655376 | tf_op jit(solution)/shard_map/reduce_sum | solution.py:70
  321.2 6.6 collective-permute-done.9
  328.5 22.5 %all-reduce.40 = (f32[4]{0:T(128)S(1)}, f32[4]{0:T(128)S(1)}) all-reduce(f32[4]{0:T(128)S(1)} %fusion, f32[4]{0:T(128)S(1)} %get-tuple-element.19), channel_id=1, replica_groups=mesh['src'=16,'dom'=16] {'dom'}, use_global_device_ids=true, to_apply=%region_15.16 | all-reduce | flops 8 | bytes 64 | tf_op jit(solution)/shard_map/psum | solution.py:78
  351.3 25.9 %psum.107 = f32[4]{0:T(128)S(1)} all-reduce(f32[4]{0:T(128)S(1)} %get-tuple-element.17), channel_id=1, replica_groups=mesh['src'=16,'dom'=16] {'dom'}, use_global_device_ids=true, to_apply=%region_19.20 | all-reduce | flops 4 | bytes 32 | tf_op jit(solution)/shard_map/psum | solution.py:78
  377.5 5.7 collective-permute-start.10
  385.4 3.5 collective-permute-done.10
  388.9 5.6 collective-permute-done.11
  395.2 22.3 %psum.108 = f32[4]{0:T(128)S(1)} all-reduce(f32[4]{0:T(128)S(1)} %get-tuple-element.15), channel_id=1, replica_groups=mesh['src'=16,'dom'=16] {'dom'}, use_global_device_ids=true, to_apply=%region_21.22 | all-reduce | flops 4 | bytes 32 | tf_op jit(solution)/shard_map/psum | solution.py:78
  418.9 25.8 %psum.109 = f32[4]{0:T(128)} all-reduce(f32[4]{0:T(128)S(1)} %multiply_reduce_fusion), channel_id=1, replica_groups=mesh['src'=16,'dom'=16] {'dom'}, use_global_device_ids=true, to_apply=%region_23.24 | all-reduce | flops 4 | bytes 32 | tf_op jit(solution)/shard_map/psum | solution.py:78
  446.7 5.7 collective-permute-start.12
  454.6 3.5 collective-permute-done.12
  458.1 5.6 collective-permute-done.13
  465.3 22.3 %psum.110 = f32[4]{0:T(128)S(1)} all-reduce(f32[4]{0:T(128)S(1)} %fusion.65), channel_id=1, replica_groups=mesh['src'=16,'dom'=16] {'dom'}, use_global_device_ids=true, to_apply=%region_25.26 | all-reduce | flops 4 | bytes 32 | tf_op jit(solution)/shard_map/psum | solution.py:78
  495.2 161.3 %all-reduce.44.cloned.1.call-done = f32[3,2,128,128]{3,2,1,0:T(8,128)} async-done(((f32[3,2,128,128]{3,2,1,0:T(8,128)}), f32[3,2,128,128]{3,2,1,0:T(8,128)}) %all-reduce.44.cloned.1.call-update) | async-done | bytes 393232 | tf_op jit(solution)/shard_map/psum | solution.py:166
  (158 shorter events, 66.6 us)
Async XLA Ops:
  7.2 649.3 %all-reduce.44.cloned.1.call-start = ((), (), s32[]{:S(2)}) async-start(), calls=%async_computation | async-start | bytes 786432 | tf_op jit(solution)/shard_map/psum | solution.py:166
  9.4 12.3 %collective-permute-start.1 = (f32[5,1,128,128]{3,2,1,0:T(8,128)S(1)}, f32[5,1,128,128]{3,2,1,0:T(8,128)S(1)}, u32[]{:S(2)}, u32[]{:S(2)}) collective-permute-start(f32[5,1,128,128]{3,2,1,0:T(8,128)S(1)} %get-tuple-element.37), channel_id=1, source_target_pairs={{0,1},{1,2},{2,3},{3,4},{4,5},{5,6},{6,7},{7,8},{8,9},{9,10},{10,1... | collective-permute-start | bytes 983048 | tf_op jit(solution)/shard_map/ppermute | solution.py:14
  11.3 10.4 %collective-permute-start = (f32[5,1,128,128]{3,2,1,0:T(8,128)S(1)}, f32[5,1,128,128]{3,2,1,0:T(8,128)S(1)}, u32[]{:S(2)}, u32[]{:S(2)}) collective-permute-start(f32[5,1,128,128]{3,2,1,0:T(8,128)S(1)} %get-tuple-element.38), channel_id=1, source_target_pairs={{1,0},{2,1},{3,2},{4,3},{5,4},{6,5},{7,6},{8,7},{9,8},{10,9},{11,1... | collective-permute-start | bytes 983048 | tf_op jit(solution)/shard_map/ppermute | solution.py:17
  21.7 40.2 %copy-start.4 = (f32[5,1,128,128]{3,2,1,0:T(8,128)}, f32[5,1,128,128]{3,2,1,0:T(8,128)S(1)}, u32[]{:S(2)}) copy-start(f32[5,1,128,128]{3,2,1,0:T(8,128)S(1)} %collective-permute-done.1) | copy-start | bytes 983044
  23.1 105.7 %copy-start.27 = (s32[1,1024]{1,0:T(1,128)S(1)}, s32[1,1024]{1,0:T(1,128)}, u32[]{:S(2)}) copy-start(s32[1,1024]{1,0:T(1,128)} %param.7) | copy-start | bytes 12292
  26.8 7.9 %collective-permute-start.2 = (f32[4,1,128,128]{3,2,1,0:T(8,128)S(1)}, f32[4,1,128,128]{3,2,1,0:T(8,128)S(1)}, u32[]{:S(2)}, u32[]{:S(2)}) collective-permute-start(f32[4,1,128,128]{3,2,1,0:T(8,128)S(1)} %get-tuple-element.77), channel_id=1, source_target_pairs={{1,0},{2,1},{3,2},{4,3},{5,4},{6,5},{7,6},{8,7},{9,8},{10,9},{11,1... | collective-permute-start | bytes 786440 | tf_op jit(solution)/shard_map/ppermute | solution.py:17
  30.1 169.6 %copy-start = (f32[1,4,2,128,128]{4,3,2,1,0:T(8,128)S(1)}, f32[1,4,2,128,128]{4,3,2,1,0:T(8,128)}, u32[]{:S(2)}) copy-start(f32[1,4,2,128,128]{4,3,2,1,0:T(8,128)} %param.4) | copy-start | bytes 1572868
  30.1 8.7 %collective-permute-start.3 = (f32[4,1,128,128]{3,2,1,0:T(8,128)S(1)}, f32[4,1,128,128]{3,2,1,0:T(8,128)S(1)}, u32[]{:S(2)}, u32[]{:S(2)}) collective-permute-start(f32[4,1,128,128]{3,2,1,0:T(8,128)S(1)} %get-tuple-element.78), channel_id=1, source_target_pairs={{0,1},{1,2},{2,3},{3,4},{4,5},{5,6},{6,7},{7,8},{8,9},{9,10},{10,1... | collective-permute-start | bytes 786440 | tf_op jit(solution)/shard_map/ppermute | solution.py:14
  61.9 41.4 %copy-start.30 = (f32[4]{0:T(128)}, f32[4]{0:T(128)S(1)}, u32[]{:S(2)}) copy-start(f32[4]{0:T(128)S(1)} %div.98) | copy-start | bytes 52
  86.9 10.8 %collective-permute-start.4 = (f32[4,1,128,128]{3,2,1,0:T(8,128)S(1)}, f32[4,1,128,128]{3,2,1,0:T(8,128)S(1)}, u32[]{:S(2)}, u32[]{:S(2)}) collective-permute-start(f32[4,1,128,128]{3,2,1,0:T(8,128)S(1)} %get-tuple-element.71), channel_id=1, source_target_pairs={{1,0},{2,1},{3,2},{4,3},{5,4},{6,5},{7,6},{8,7},{9,8},{10,9},{11,1... | collective-permute-start | bytes 786440 | tf_op jit(solution)/shard_map/ppermute | solution.py:17
  92.0 11.3 %collective-permute-start.5 = (f32[4,1,128,128]{3,2,1,0:T(8,128)S(1)}, f32[4,1,128,128]{3,2,1,0:T(8,128)S(1)}, u32[]{:S(2)}, u32[]{:S(2)}) collective-permute-start(f32[4,1,128,128]{3,2,1,0:T(8,128)S(1)} %get-tuple-element.72), channel_id=1, source_target_pairs={{0,1},{1,2},{2,3},{3,4},{4,5},{5,6},{6,7},{7,8},{8,9},{9,10},{10,1... | collective-permute-start | bytes 786440 | tf_op jit(solution)/shard_map/ppermute | solution.py:14
  104.0 50.7 %copy-start.3 = (f32[4,2,128,128]{3,2,1,0:T(8,128)}, f32[4,2,128,128]{3,2,1,0:T(8,128)S(1)}, u32[]{:S(2)}) copy-start(f32[4,2,128,128]{3,2,1,0:T(8,128)S(1)} %get-tuple-element.22) | copy-start | bytes 1572868
  156.6 11.4 %collective-permute-start.6 = (f32[4,1,128,128]{3,2,1,0:T(8,128)S(1)}, f32[4,1,128,128]{3,2,1,0:T(8,128)S(1)}, u32[]{:S(2)}, u32[]{:S(2)}) collective-permute-start(f32[4,1,128,128]{3,2,1,0:T(8,128)S(1)} %get-tuple-element.65), channel_id=1, source_target_pairs={{1,0},{2,1},{3,2},{4,3},{5,4},{6,5},{7,6},{8,7},{9,8},{10,9},{11,1... | collective-permute-start | bytes 786440 | tf_op jit(solution)/shard_map/ppermute | solution.py:17
  162.4 11.3 %collective-permute-start.7 = (f32[4,1,128,128]{3,2,1,0:T(8,128)S(1)}, f32[4,1,128,128]{3,2,1,0:T(8,128)S(1)}, u32[]{:S(2)}, u32[]{:S(2)}) collective-permute-start(f32[4,1,128,128]{3,2,1,0:T(8,128)S(1)} %get-tuple-element.66), channel_id=1, source_target_pairs={{0,1},{1,2},{2,3},{3,4},{4,5},{5,6},{6,7},{7,8},{8,9},{9,10},{10,1... | collective-permute-start | bytes 786440 | tf_op jit(solution)/shard_map/ppermute | solution.py:14
  200.4 74.1 %copy-start.8 = (f32[1,4,1024]{1,2,0:T(8,128)S(1)}, f32[1,4,1024]{1,2,0:T(8,128)}, u32[]{:S(2)}) copy-start(f32[1,4,1024]{1,2,0:T(8,128)} %copy.12) | copy-start | bytes 49156
  288.0 30.2 %copy-start.5 = (f32[5,1,128,128]{3,2,1,0:T(8,128)S(1)}, f32[5,1,128,128]{3,2,1,0:T(8,128)}, u32[]{:S(2)}) copy-start(f32[5,1,128,128]{3,2,1,0:T(8,128)} %copy-done.4) | copy-start | bytes 983044
  288.0 30.2 %copy-start.7 = (f32[5,1,128,128]{3,2,1,0:T(8,128)S(1)}, f32[5,1,128,128]{3,2,1,0:T(8,128)}, u32[]{:S(2)}) copy-start(f32[5,1,128,128]{3,2,1,0:T(8,128)} %copy-done.6) | copy-start | bytes 983044
  288.0 30.2 %copy-start.16 = (f32[4,1,128,128]{3,2,1,0:T(8,128)S(1)}, f32[4,1,128,128]{3,2,1,0:T(8,128)}, u32[]{:S(2)}) copy-start(f32[4,1,128,128]{3,2,1,0:T(8,128)} %copy-done.15) | copy-start | bytes 786436
  288.0 30.2 %copy-start.18 = (f32[4,1,128,128]{3,2,1,0:T(8,128)S(1)}, f32[4,1,128,128]{3,2,1,0:T(8,128)}, u32[]{:S(2)}) copy-start(f32[4,1,128,128]{3,2,1,0:T(8,128)} %copy-done.17) | copy-start | bytes 786436
  288.0 30.2 %copy-start.20 = (f32[4,1,128,128]{3,2,1,0:T(8,128)S(1)}, f32[4,1,128,128]{3,2,1,0:T(8,128)}, u32[]{:S(2)}) copy-start(f32[4,1,128,128]{3,2,1,0:T(8,128)} %copy-done.19) | copy-start | bytes 786436
  288.0 30.2 %copy-start.29 = (f32[4]{0:T(128)S(1)}, f32[4]{0:T(128)}, u32[]{:S(2)}) copy-start(f32[4]{0:T(128)} %copy-done.28) | copy-start | bytes 52
  288.0 30.2 %copy-start.31 = (f32[4]{0:T(128)S(1)}, f32[4]{0:T(128)}, u32[]{:S(2)}) copy-start(f32[4]{0:T(128)} %copy-done.30) | copy-start | bytes 52
  298.1 20.1 %copy-start.22 = (f32[4,1,128,128]{3,2,1,0:T(8,128)S(1)}, f32[4,1,128,128]{3,2,1,0:T(8,128)}, u32[]{:S(2)}) copy-start(f32[4,1,128,128]{3,2,1,0:T(8,128)} %copy-done.21) | copy-start | bytes 786436
  298.1 20.1 %copy-start.24 = (f32[4,1,128,128]{3,2,1,0:T(8,128)S(1)}, f32[4,1,128,128]{3,2,1,0:T(8,128)}, u32[]{:S(2)}) copy-start(f32[4,1,128,128]{3,2,1,0:T(8,128)} %copy-done.23) | copy-start | bytes 786436
  298.1 20.1 %copy-start.26 = (f32[4,1,128,128]{3,2,1,0:T(8,128)S(1)}, f32[4,1,128,128]{3,2,1,0:T(8,128)}, u32[]{:S(2)}) copy-start(f32[4,1,128,128]{3,2,1,0:T(8,128)} %copy-done.25) | copy-start | bytes 786436
  313.8 7.4 %collective-permute-start.8 = (f32[4,1,128,128]{3,2,1,0:T(8,128)S(1)}, f32[4,1,128,128]{3,2,1,0:T(8,128)S(1)}, u32[]{:S(2)}, u32[]{:S(2)}) collective-permute-start(f32[4,1,128,128]{3,2,1,0:T(8,128)S(1)} %get-tuple-element.59), channel_id=1, source_target_pairs={{1,0},{2,1},{3,2},{4,3},{5,4},{6,5},{7,6},{8,7},{9,8},{10,9},{11,1... | collective-permute-start | bytes 786440 | tf_op jit(solution)/shard_map/ppermute | solution.py:17
  316.0 11.8 %collective-permute-start.9 = (f32[4,1,128,128]{3,2,1,0:T(8,128)S(1)}, f32[4,1,128,128]{3,2,1,0:T(8,128)S(1)}, u32[]{:S(2)}, u32[]{:S(2)}) collective-permute-start(f32[4,1,128,128]{3,2,1,0:T(8,128)S(1)} %get-tuple-element.60), channel_id=1, source_target_pairs={{0,1},{1,2},{2,3},{3,4},{4,5},{5,6},{6,7},{7,8},{8,9},{9,10},{10,1... | collective-permute-start | bytes 786440 | tf_op jit(solution)/shard_map/ppermute | solution.py:14
  377.5 11.4 %collective-permute-start.10 = (f32[4,1,128,128]{3,2,1,0:T(8,128)S(1)}, f32[4,1,128,128]{3,2,1,0:T(8,128)S(1)}, u32[]{:S(2)}, u32[]{:S(2)}) collective-permute-start(f32[4,1,128,128]{3,2,1,0:T(8,128)S(1)} %get-tuple-element.53), channel_id=1, source_target_pairs={{1,0},{2,1},{3,2},{4,3},{5,4},{6,5},{7,6},{8,7},{9,8},{10,9},{11,1... | collective-permute-start | bytes 786440 | tf_op jit(solution)/shard_map/ppermute | solution.py:17
  383.2 11.3 %collective-permute-start.11 = (f32[4,1,128,128]{3,2,1,0:T(8,128)S(1)}, f32[4,1,128,128]{3,2,1,0:T(8,128)S(1)}, u32[]{:S(2)}, u32[]{:S(2)}) collective-permute-start(f32[4,1,128,128]{3,2,1,0:T(8,128)S(1)} %get-tuple-element.54), channel_id=1, source_target_pairs={{0,1},{1,2},{2,3},{3,4},{4,5},{5,6},{6,7},{7,8},{8,9},{9,10},{10,1... | collective-permute-start | bytes 786440 | tf_op jit(solution)/shard_map/ppermute | solution.py:14
  395.2 49.4 %copy-start.2 = (f32[4,2,128,128]{3,2,1,0:T(8,128)}, f32[4,2,128,128]{3,2,1,0:T(8,128)S(1)}, u32[]{:S(2)}) copy-start(f32[4,2,128,128]{3,2,1,0:T(8,128)S(1)} %get-tuple-element.16) | copy-start | bytes 1572868
  446.7 11.4 %collective-permute-start.12 = (f32[4,1,128,128]{3,2,1,0:T(8,128)S(1)}, f32[4,1,128,128]{3,2,1,0:T(8,128)S(1)}, u32[]{:S(2)}, u32[]{:S(2)}) collective-permute-start(f32[4,1,128,128]{3,2,1,0:T(8,128)S(1)} %get-tuple-element.47), channel_id=1, source_target_pairs={{1,0},{2,1},{3,2},{4,3},{5,4},{6,5},{7,6},{8,7},{9,8},{10,9},{11,1... | collective-permute-start | bytes 786440 | tf_op jit(solution)/shard_map/ppermute | solution.py:17
  452.4 11.3 %collective-permute-start.13 = (f32[4,1,128,128]{3,2,1,0:T(8,128)S(1)}, f32[4,1,128,128]{3,2,1,0:T(8,128)S(1)}, u32[]{:S(2)}, u32[]{:S(2)}) collective-permute-start(f32[4,1,128,128]{3,2,1,0:T(8,128)S(1)} %get-tuple-element.48), channel_id=1, source_target_pairs={{0,1},{1,2},{2,3},{3,4},{4,5},{5,6},{6,7},{7,8},{8,9},{9,10},{10,1... | collective-permute-start | bytes 786440 | tf_op jit(solution)/shard_map/ppermute | solution.py:14
  (16 other events, 74.0 us)
Sparse Core Ops, SparseCore 0:
  493.5 162.9 all-reduce.43
where the time goes:
time: 666 us; the launch traced here: 665 us
  blocking collectives  292 us (44%)
  waiting for transfers between devices  213 us (32%)
  other arithmetic  56.5 us (8%)
  starting transfers between devices  46.1 us (7%)
  local copies, waits for them, and re-layouts  42.4 us (6%)
  between operations  14.7 us (2%)
    psum x10, blocking collectives, summed(): return lax.psum(values, 'dom')  236 us
    psum x1, waiting for transfers between devices, per_device(): summed_grad = lax.psum(local_grad, 'src')  161 us
    psum x1, blocking collectives, per_device(): predicted = lax.psum(picked, 'dom')  55.9 us
    ppermute x7, waiting for transfers between devices, extended_2(): lax.ppermute(lax.slice_in_dim(block, block.shape[dim] - width, None, axis...  33.2 us
    ppermute x7, starting transfers between devices, extended_2(): lax.ppermute(lax.slice_in_dim(block, 0, width, axis=dim), axis, backward)  32.3 us
    reduce_sum x11, other arithmetic, local_inner(): return jnp.sum(left * right, axis=(1, 2, 3))  20.7 us
    ppermute x7, waiting for transfers between devices, extended_2(): lax.ppermute(lax.slice_in_dim(block, 0, width, axis=dim), axis, backward)  18.5 us
    ppermute x7, starting transfers between devices, extended_2(): lax.ppermute(lax.slice_in_dim(block, block.shape[dim] - width, None, axis...  13.8 us
  transfers between devices with their start and end apart: 15, of which 13 were waited for; matrix products, arithmetic and copies ran while one was open for 1% of the time, Pallas kernels for 0%

commit v1 on v0

--- a/solution.py
+++ b/solution.py
@@ -163,7 +163,7 @@
         )
         pieces.append(-0.5 * jnp.sum(upper_term + lower_term, axis=0))
     local_grad = jnp.stack(pieces)
-    summed_grad = lax.psum(local_grad, "src")
+    summed_grad = jnp.sum(lax.all_gather(local_grad, "src"), axis=0)
     return (summed_grad, predicted[None])
 
 

time: 666 us -> 627 us (0.941)
  waiting for transfers between devices: 213 us -> 171 us
    psum x1 -> x0, waiting for transfers between devices: 161 us -> none  [per_device(): summed_grad = lax.psum(local_grad, 'src')]
    all_gather x0 -> x1, waiting for transfers between devices: none -> 119 us  [per_device(): summed_grad = jnp.sum(lax.all_gather(local_grad, 'src'), axis=0)]
  transfers between devices with their start and end apart: 15 -> 15, of which waited for: 13 -> 13; matrix products, arithmetic and copies ran while one was open for 1% -> 2% of each run, Pallas kernels for 0% -> 0%
where the time goes in v1:
time: 627 us; the launch traced here: 625 us
  blocking collectives  292 us (47%)
  waiting for transfers between devices  171 us (27%)
  other arithmetic  60.4 us (10%)
  starting transfers between devices  46.1 us (7%)
  local copies, waits for them, and re-layouts  40.7 us (6%)
  between operations  14.7 us (2%)
    psum x10, blocking collectives, summed(): return lax.psum(values, 'dom')  236 us
    all_gather x1, waiting for transfers between devices, per_device(): summed_grad = jnp.sum(lax.all_gather(local_grad, 'src'), axis=0)  119 us
    psum x1, blocking collectives, per_device(): predicted = lax.psum(picked, 'dom')  55.9 us
    ppermute x7, waiting for transfers between devices, extended_2(): lax.ppermute(lax.slice_in_dim(block, block.shape[dim] - width, None, axis...  33.2 us
    ppermute x7, starting transfers between devices, extended_2(): lax.ppermute(lax.slice_in_dim(block, 0, width, axis=dim), axis, backward)  32.3 us
    reduce_sum x11, other arithmetic, local_inner(): return jnp.sum(left * right, axis=(1, 2, 3))  20.7 us
    ppermute x7, waiting for transfers between devices, extended_2(): lax.ppermute(lax.slice_in_dim(block, 0, width, axis=dim), axis, backward)  18.5 us
    ppermute x7, starting transfers between devices, extended_2(): lax.ppermute(lax.slice_in_dim(block, block.shape[dim] - width, None, axis...  13.8 us
  transfers between devices with their start and end apart: 15, of which 13 were waited for; matrix products, arithmetic and copies ran while one was open for 2% of the time, Pallas kernels for 0%

profile of v1, /device:TPU:8, one launch (start us, length us, event | category | flops | bytes accessed | tf_op | source)
XLA Modules:
  0.0 625.3 jit_solution(2064485535595949291)
XLA Ops:
  11.3 4.5 collective-permute-start
  34.7 4.1 collective-permute-done.3
  39.5 22.3 %all-reduce.41 = (f32[4]{0:T(128)S(1)}, f32[4]{0:T(128)S(1)}) all-reduce(f32[4]{0:T(128)S(1)} %get-tuple-element.12, f32[4]{0:T(128)S(1)} %get-tuple-element.11), channel_id=1, replica_groups=mesh['src'=16,'dom'=16] {'dom'}, use_global_device_ids=true, to_apply=%region_1.2 | all-reduce | flops 8 | bytes 64 | tf_op jit(solution)/shard_map/psum | solution.py:78
  62.1 24.5 %psum.93 = f32[4]{0:T(128)S(1)} all-reduce(f32[4]{0:T(128)S(1)} %get-tuple-element.25), channel_id=1, replica_groups=mesh['src'=16,'dom'=16] {'dom'}, use_global_device_ids=true, to_apply=%region_5.6 | all-reduce | flops 4 | bytes 32 | tf_op jit(solution)/shard_map/psum | solution.py:78
  86.9 5.1 collective-permute-start.4
  94.1 3.5 collective-permute-done.4
  97.6 5.6 collective-permute-done.5
  104.0 22.9 %psum.94 = f32[4]{0:T(128)} all-reduce(f32[4]{0:T(128)S(1)} %get-tuple-element.23), channel_id=1, replica_groups=mesh['src'=16,'dom'=16] {'dom'}, use_global_device_ids=true, to_apply=%region_7.8 | all-reduce | flops 4 | bytes 32 | tf_op jit(solution)/shard_map/psum | solution.py:78
  128.9 25.8 %psum.95 = f32[4]{0:T(128)} all-reduce(f32[4]{0:T(128)} %multiply_reduce_fusion.4), channel_id=1, replica_groups=mesh['src'=16,'dom'=16] {'dom'}, use_global_device_ids=true, to_apply=%region_9.10 | all-reduce | flops 4 | bytes 32 | tf_op jit(solution)/shard_map/psum | solution.py:78
  156.6 5.7 collective-permute-start.6
  164.5 3.5 collective-permute-done.6
  168.0 5.6 collective-permute-done.7
  176.7 22.3 %psum.96 = f32[4]{0:T(128)S(1)} all-reduce(f32[4]{0:T(128)S(1)} %fusion.64), channel_id=1, replica_groups=mesh['src'=16,'dom'=16] {'dom'}, use_global_device_ids=true, to_apply=%region_11.12 | all-reduce | flops 4 | bytes 32 | tf_op jit(solution)/shard_map/psum | solution.py:78
  200.5 8.6 %copy.16 = f32[4,2,128,128]{0,3,2,1:T(8,128)} copy(f32[4,2,128,128]{3,2,1,0:T(8,128)S(1)} %add_add_fusion) | data formatting | bytes 1048576 | tf_op jit(solution)/shard_map/add | solution.py:136
  209.1 8.6 %gather_fusion = f32[1024,4]{1,0:T(8,128)S(1)} fusion(f32[4,32768]{0,1:T(8,128)} %bitcast.79, s32[1024]{0:T(1024)S(1)} %broadcast_clamp_fusion), kind=kCustom, calls=%fused_computation | custom fusion | bytes 36864 | tf_op jit(solution)/shard_map/jit(_take)/gather | solution.py:147
  218.7 55.9 %psum.97 = f32[4,1024]{0,1:T(8,128)S(1)} all-reduce(f32[4,1024]{0,1:T(8,128)S(1)} %select_bitcast_fusion), channel_id=1, replica_groups=mesh['src'=16,'dom'=16] {'dom'}, use_global_device_ids=true, to_apply=%region_12.13 | all-reduce | flops 4096 | bytes 32768 | tf_op jit(solution)/shard_map/psum | solution.py:148
  274.6 13.4 %scatter_custom_fusion = f32[4,32768]{0,1:T(8,128)} fusion(s32[1024]{0:T(1024)S(1)} %bitcast.84, f32[]{:T(128)} %constant.79.clone.1, f32[4,1024]{0,1:T(8,128)S(1)} %psum.97, f32[1,4,1024]{1,2,0:T(8,128)S(1)} %copy-done.8, pred[1024]{0:T(1024)(128)(4,1)S(1)} %and_reduce_fusion), kind=kCustom, calls=%fused_computation.4 | custom fusion | flops 12288 | bytes 1574912 | tf_op jit(solution)/shard_map/scatter-add | solution.py:150
  288.0 10.1 %copy.18 = f32[4,2,128,128]{3,2,1,0:T(8,128)S(1)} copy(f32[4,2,128,128]{0,3,2,1:T(8,128)} %bitcast.72) | data formatting | bytes 1048576 | tf_op jit(solution)/shard_map/reshape | solution.py:150
  298.5 15.3 %fusion = f32[4]{0:T(128)S(1)} fusion(f32[4,32768]{0,1:T(8,128)} %scatter_custom_fusion, f32[32768]{0:T(1024)S(1)} %bitcast.73), kind=kLoop, calls=%fused_computation.3 | loop fusion | flops 393212 | bytes 655376 | tf_op jit(solution)/shard_map/reduce_sum | solution.py:70
  321.2 6.6 %collective-permute-done.9 = f32[4,1,128,128]{3,2,1,0:T(8,128)S(1)} collective-permute-done((f32[4,1,128,128]{3,2,1,0:T(8,128)S(1)}, f32[4,1,128,128]{3,2,1,0:T(8,128)S(1)}, u32[]{:S(2)}, u32[]{:S(2)}) %collective-permute-start.9) | collective-permute-done | bytes 262176 | tf_op jit(solution)/shard_map/ppermute | solution.py:14
  328.5 22.5 %all-reduce.40 = (f32[4]{0:T(128)S(1)}, f32[4]{0:T(128)S(1)}) all-reduce(f32[4]{0:T(128)S(1)} %fusion, f32[4]{0:T(128)S(1)} %get-tuple-element.21), channel_id=1, replica_groups=mesh['src'=16,'dom'=16] {'dom'}, use_global_device_ids=true, to_apply=%region_15.16 | all-reduce | flops 8 | bytes 64 | tf_op jit(solution)/shard_map/psum | solution.py:78
  351.3 25.9 %psum.100 = f32[4]{0:T(128)S(1)} all-reduce(f32[4]{0:T(128)S(1)} %get-tuple-element.19), channel_id=1, replica_groups=mesh['src'=16,'dom'=16] {'dom'}, use_global_device_ids=true, to_apply=%region_19.20 | all-reduce | flops 4 | bytes 32 | tf_op jit(solution)/shard_map/psum | solution.py:78
  377.5 5.7 collective-permute-start.10
  385.4 3.5 collective-permute-done.10
  388.9 5.6 collective-permute-done.11
  395.2 22.3 %psum.101 = f32[4]{0:T(128)S(1)} all-reduce(f32[4]{0:T(128)S(1)} %get-tuple-element.17), channel_id=1, replica_groups=mesh['src'=16,'dom'=16] {'dom'}, use_global_device_ids=true, to_apply=%region_21.22 | all-reduce | flops 4 | bytes 32 | tf_op jit(solution)/shard_map/psum | solution.py:78
  418.9 25.8 %psum.102 = f32[4]{0:T(128)} all-reduce(f32[4]{0:T(128)S(1)} %multiply_reduce_fusion), channel_id=1, replica_groups=mesh['src'=16,'dom'=16] {'dom'}, use_global_device_ids=true, to_apply=%region_23.24 | all-reduce | flops 4 | bytes 32 | tf_op jit(solution)/shard_map/psum | solution.py:78
  446.7 5.7 collective-permute-start.12
  458.1 5.6 collective-permute-done.13
  465.3 22.3 %psum.103 = f32[4]{0:T(128)S(1)} all-reduce(f32[4]{0:T(128)S(1)} %fusion.65), channel_id=1, replica_groups=mesh['src'=16,'dom'=16] {'dom'}, use_global_device_ids=true, to_apply=%region_25.26 | all-reduce | flops 4 | bytes 32 | tf_op jit(solution)/shard_map/psum | solution.py:78
  495.2 119.3 %all-gather.3.cloned.1.call-done = f32[48,2,128,128]{3,2,1,0:T(8,128)} async-done(((f32[3,2,128,128]{3,2,1,0:T(8,128)}), f32[48,2,128,128]{3,2,1,0:T(8,128)}) %all-gather.3.cloned.1.call-update) | async-done | bytes 6291472 | tf_op jit(solution)/shard_map/all_gather | solution.py:166
  614.5 3.9 reduce_sum.159
  (158 shorter events, 68.3 us)
Async XLA Ops:
  7.2 607.4 %all-gather.3.cloned.1.call-start = ((), (), s32[]{:S(2)}) async-start(), calls=%async_computation | async-start | bytes 6684672 | tf_op jit(solution)/shard_map/all_gather | solution.py:166
  9.4 12.3 %collective-permute-start.1 = (f32[5,1,128,128]{3,2,1,0:T(8,128)S(1)}, f32[5,1,128,128]{3,2,1,0:T(8,128)S(1)}, u32[]{:S(2)}, u32[]{:S(2)}) collective-permute-start(f32[5,1,128,128]{3,2,1,0:T(8,128)S(1)} %get-tuple-element.39), channel_id=1, source_target_pairs={{0,1},{1,2},{2,3},{3,4},{4,5},{5,6},{6,7},{7,8},{8,9},{9,10},{10,1... | collective-permute-start | bytes 983048 | tf_op jit(solution)/shard_map/ppermute | solution.py:14
  11.3 10.4 %collective-permute-start = (f32[5,1,128,128]{3,2,1,0:T(8,128)S(1)}, f32[5,1,128,128]{3,2,1,0:T(8,128)S(1)}, u32[]{:S(2)}, u32[]{:S(2)}) collective-permute-start(f32[5,1,128,128]{3,2,1,0:T(8,128)S(1)} %get-tuple-element.40), channel_id=1, source_target_pairs={{1,0},{2,1},{3,2},{4,3},{5,4},{6,5},{7,6},{8,7},{9,8},{10,9},{11,1... | collective-permute-start | bytes 983048 | tf_op jit(solution)/shard_map/ppermute | solution.py:17
  21.7 40.2 %copy-start.4 = (f32[5,1,128,128]{3,2,1,0:T(8,128)}, f32[5,1,128,128]{3,2,1,0:T(8,128)S(1)}, u32[]{:S(2)}) copy-start(f32[5,1,128,128]{3,2,1,0:T(8,128)S(1)} %collective-permute-done.1) | copy-start | bytes 983044
  23.1 105.7 %copy-start.27 = (s32[1,1024]{1,0:T(1,128)S(1)}, s32[1,1024]{1,0:T(1,128)}, u32[]{:S(2)}) copy-start(s32[1,1024]{1,0:T(1,128)} %param.7) | copy-start | bytes 12292
  26.8 7.9 %collective-permute-start.2 = (f32[4,1,128,128]{3,2,1,0:T(8,128)S(1)}, f32[4,1,128,128]{3,2,1,0:T(8,128)S(1)}, u32[]{:S(2)}, u32[]{:S(2)}) collective-permute-start(f32[4,1,128,128]{3,2,1,0:T(8,128)S(1)} %get-tuple-element.79), channel_id=1, source_target_pairs={{1,0},{2,1},{3,2},{4,3},{5,4},{6,5},{7,6},{8,7},{9,8},{10,9},{11,1... | collective-permute-start | bytes 786440 | tf_op jit(solution)/shard_map/ppermute | solution.py:17
  30.1 169.6 %copy-start = (f32[1,4,2,128,128]{4,3,2,1,0:T(8,128)S(1)}, f32[1,4,2,128,128]{4,3,2,1,0:T(8,128)}, u32[]{:S(2)}) copy-start(f32[1,4,2,128,128]{4,3,2,1,0:T(8,128)} %param.4) | copy-start | bytes 1572868
  30.1 8.7 %collective-permute-start.3 = (f32[4,1,128,128]{3,2,1,0:T(8,128)S(1)}, f32[4,1,128,128]{3,2,1,0:T(8,128)S(1)}, u32[]{:S(2)}, u32[]{:S(2)}) collective-permute-start(f32[4,1,128,128]{3,2,1,0:T(8,128)S(1)} %get-tuple-element.80), channel_id=1, source_target_pairs={{0,1},{1,2},{2,3},{3,4},{4,5},{5,6},{6,7},{7,8},{8,9},{9,10},{10,1... | collective-permute-start | bytes 786440 | tf_op jit(solution)/shard_map/ppermute | solution.py:14
  61.9 41.4 %copy-start.30 = (f32[4]{0:T(128)}, f32[4]{0:T(128)S(1)}, u32[]{:S(2)}) copy-start(f32[4]{0:T(128)S(1)} %div.98) | copy-start | bytes 52
  86.9 10.8 %collective-permute-start.4 = (f32[4,1,128,128]{3,2,1,0:T(8,128)S(1)}, f32[4,1,128,128]{3,2,1,0:T(8,128)S(1)}, u32[]{:S(2)}, u32[]{:S(2)}) collective-permute-start(f32[4,1,128,128]{3,2,1,0:T(8,128)S(1)} %get-tuple-element.73), channel_id=1, source_target_pairs={{1,0},{2,1},{3,2},{4,3},{5,4},{6,5},{7,6},{8,7},{9,8},{10,9},{11,1... | collective-permute-start | bytes 786440 | tf_op jit(solution)/shard_map/ppermute | solution.py:17
  92.0 11.3 %collective-permute-start.5 = (f32[4,1,128,128]{3,2,1,0:T(8,128)S(1)}, f32[4,1,128,128]{3,2,1,0:T(8,128)S(1)}, u32[]{:S(2)}, u32[]{:S(2)}) collective-permute-start(f32[4,1,128,128]{3,2,1,0:T(8,128)S(1)} %get-tuple-element.74), channel_id=1, source_target_pairs={{0,1},{1,2},{2,3},{3,4},{4,5},{5,6},{6,7},{7,8},{8,9},{9,10},{10,1... | collective-permute-start | bytes 786440 | tf_op jit(solution)/shard_map/ppermute | solution.py:14
  104.0 50.7 %copy-start.3 = (f32[4,2,128,128]{3,2,1,0:T(8,128)}, f32[4,2,128,128]{3,2,1,0:T(8,128)S(1)}, u32[]{:S(2)}) copy-start(f32[4,2,128,128]{3,2,1,0:T(8,128)S(1)} %get-tuple-element.24) | copy-start | bytes 1572868
  156.6 11.4 %collective-permute-start.6 = (f32[4,1,128,128]{3,2,1,0:T(8,128)S(1)}, f32[4,1,128,128]{3,2,1,0:T(8,128)S(1)}, u32[]{:S(2)}, u32[]{:S(2)}) collective-permute-start(f32[4,1,128,128]{3,2,1,0:T(8,128)S(1)} %get-tuple-element.67), channel_id=1, source_target_pairs={{1,0},{2,1},{3,2},{4,3},{5,4},{6,5},{7,6},{8,7},{9,8},{10,9},{11,1... | collective-permute-start | bytes 786440 | tf_op jit(solution)/shard_map/ppermute | solution.py:17
  162.4 11.3 %collective-permute-start.7 = (f32[4,1,128,128]{3,2,1,0:T(8,128)S(1)}, f32[4,1,128,128]{3,2,1,0:T(8,128)S(1)}, u32[]{:S(2)}, u32[]{:S(2)}) collective-permute-start(f32[4,1,128,128]{3,2,1,0:T(8,128)S(1)} %get-tuple-element.68), channel_id=1, source_target_pairs={{0,1},{1,2},{2,3},{3,4},{4,5},{5,6},{6,7},{7,8},{8,9},{9,10},{10,1... | collective-permute-start | bytes 786440 | tf_op jit(solution)/shard_map/ppermute | solution.py:14
  200.4 74.1 %copy-start.8 = (f32[1,4,1024]{1,2,0:T(8,128)S(1)}, f32[1,4,1024]{1,2,0:T(8,128)}, u32[]{:S(2)}) copy-start(f32[1,4,1024]{1,2,0:T(8,128)} %copy.17) | copy-start | bytes 49156
  288.0 30.2 %copy-start.5 = (f32[5,1,128,128]{3,2,1,0:T(8,128)S(1)}, f32[5,1,128,128]{3,2,1,0:T(8,128)}, u32[]{:S(2)}) copy-start(f32[5,1,128,128]{3,2,1,0:T(8,128)} %copy-done.4) | copy-start | bytes 983044
  288.0 30.2 %copy-start.7 = (f32[5,1,128,128]{3,2,1,0:T(8,128)S(1)}, f32[5,1,128,128]{3,2,1,0:T(8,128)}, u32[]{:S(2)}) copy-start(f32[5,1,128,128]{3,2,1,0:T(8,128)} %copy-done.6) | copy-start | bytes 983044
  288.0 30.2 %copy-start.16 = (f32[4,1,128,128]{3,2,1,0:T(8,128)S(1)}, f32[4,1,128,128]{3,2,1,0:T(8,128)}, u32[]{:S(2)}) copy-start(f32[4,1,128,128]{3,2,1,0:T(8,128)} %copy-done.15) | copy-start | bytes 786436
  288.0 30.2 %copy-start.18 = (f32[4,1,128,128]{3,2,1,0:T(8,128)S(1)}, f32[4,1,128,128]{3,2,1,0:T(8,128)}, u32[]{:S(2)}) copy-start(f32[4,1,128,128]{3,2,1,0:T(8,128)} %copy-done.17) | copy-start | bytes 786436
  288.0 30.2 %copy-start.20 = (f32[4,1,128,128]{3,2,1,0:T(8,128)S(1)}, f32[4,1,128,128]{3,2,1,0:T(8,128)}, u32[]{:S(2)}) copy-start(f32[4,1,128,128]{3,2,1,0:T(8,128)} %copy-done.19) | copy-start | bytes 786436
  288.0 30.2 %copy-start.29 = (f32[4]{0:T(128)S(1)}, f32[4]{0:T(128)}, u32[]{:S(2)}) copy-start(f32[4]{0:T(128)} %copy-done.28) | copy-start | bytes 52
  288.0 30.2 %copy-start.31 = (f32[4]{0:T(128)S(1)}, f32[4]{0:T(128)}, u32[]{:S(2)}) copy-start(f32[4]{0:T(128)} %copy-done.30) | copy-start | bytes 52
  298.1 20.1 %copy-start.22 = (f32[4,1,128,128]{3,2,1,0:T(8,128)S(1)}, f32[4,1,128,128]{3,2,1,0:T(8,128)}, u32[]{:S(2)}) copy-start(f32[4,1,128,128]{3,2,1,0:T(8,128)} %copy-done.21) | copy-start | bytes 786436
  298.1 20.1 %copy-start.24 = (f32[4,1,128,128]{3,2,1,0:T(8,128)S(1)}, f32[4,1,128,128]{3,2,1,0:T(8,128)}, u32[]{:S(2)}) copy-start(f32[4,1,128,128]{3,2,1,0:T(8,128)} %copy-done.23) | copy-start | bytes 786436
  298.1 20.1 %copy-start.26 = (f32[4,1,128,128]{3,2,1,0:T(8,128)S(1)}, f32[4,1,128,128]{3,2,1,0:T(8,128)}, u32[]{:S(2)}) copy-start(f32[4,1,128,128]{3,2,1,0:T(8,128)} %copy-done.25) | copy-start | bytes 786436
  313.8 7.4 %collective-permute-start.8 = (f32[4,1,128,128]{3,2,1,0:T(8,128)S(1)}, f32[4,1,128,128]{3,2,1,0:T(8,128)S(1)}, u32[]{:S(2)}, u32[]{:S(2)}) collective-permute-start(f32[4,1,128,128]{3,2,1,0:T(8,128)S(1)} %get-tuple-element.61), channel_id=1, source_target_pairs={{1,0},{2,1},{3,2},{4,3},{5,4},{6,5},{7,6},{8,7},{9,8},{10,9},{11,1... | collective-permute-start | bytes 786440 | tf_op jit(solution)/shard_map/ppermute | solution.py:17
  316.0 11.8 %collective-permute-start.9 = (f32[4,1,128,128]{3,2,1,0:T(8,128)S(1)}, f32[4,1,128,128]{3,2,1,0:T(8,128)S(1)}, u32[]{:S(2)}, u32[]{:S(2)}) collective-permute-start(f32[4,1,128,128]{3,2,1,0:T(8,128)S(1)} %get-tuple-element.62), channel_id=1, source_target_pairs={{0,1},{1,2},{2,3},{3,4},{4,5},{5,6},{6,7},{7,8},{8,9},{9,10},{10,1... | collective-permute-start | bytes 786440 | tf_op jit(solution)/shard_map/ppermute | solution.py:14
  377.5 11.4 %collective-permute-start.10 = (f32[4,1,128,128]{3,2,1,0:T(8,128)S(1)}, f32[4,1,128,128]{3,2,1,0:T(8,128)S(1)}, u32[]{:S(2)}, u32[]{:S(2)}) collective-permute-start(f32[4,1,128,128]{3,2,1,0:T(8,128)S(1)} %get-tuple-element.55), channel_id=1, source_target_pairs={{1,0},{2,1},{3,2},{4,3},{5,4},{6,5},{7,6},{8,7},{9,8},{10,9},{11,1... | collective-permute-start | bytes 786440 | tf_op jit(solution)/shard_map/ppermute | solution.py:17
  383.2 11.3 %collective-permute-start.11 = (f32[4,1,128,128]{3,2,1,0:T(8,128)S(1)}, f32[4,1,128,128]{3,2,1,0:T(8,128)S(1)}, u32[]{:S(2)}, u32[]{:S(2)}) collective-permute-start(f32[4,1,128,128]{3,2,1,0:T(8,128)S(1)} %get-tuple-element.56), channel_id=1, source_target_pairs={{0,1},{1,2},{2,3},{3,4},{4,5},{5,6},{6,7},{7,8},{8,9},{9,10},{10,1... | collective-permute-start | bytes 786440 | tf_op jit(solution)/shard_map/ppermute | solution.py:14
  395.2 49.4 %copy-start.2 = (f32[4,2,128,128]{3,2,1,0:T(8,128)}, f32[4,2,128,128]{3,2,1,0:T(8,128)S(1)}, u32[]{:S(2)}) copy-start(f32[4,2,128,128]{3,2,1,0:T(8,128)S(1)} %get-tuple-element.18) | copy-start | bytes 1572868
  446.7 11.4 %collective-permute-start.12 = (f32[4,1,128,128]{3,2,1,0:T(8,128)S(1)}, f32[4,1,128,128]{3,2,1,0:T(8,128)S(1)}, u32[]{:S(2)}, u32[]{:S(2)}) collective-permute-start(f32[4,1,128,128]{3,2,1,0:T(8,128)S(1)} %get-tuple-element.49), channel_id=1, source_target_pairs={{1,0},{2,1},{3,2},{4,3},{5,4},{6,5},{7,6},{8,7},{9,8},{10,9},{11,1... | collective-permute-start | bytes 786440 | tf_op jit(solution)/shard_map/ppermute | solution.py:17
  452.4 11.3 %collective-permute-start.13 = (f32[4,1,128,128]{3,2,1,0:T(8,128)S(1)}, f32[4,1,128,128]{3,2,1,0:T(8,128)S(1)}, u32[]{:S(2)}, u32[]{:S(2)}) collective-permute-start(f32[4,1,128,128]{3,2,1,0:T(8,128)S(1)} %get-tuple-element.50), channel_id=1, source_target_pairs={{0,1},{1,2},{2,3},{3,4},{4,5},{5,6},{6,7},{7,8},{8,9},{9,10},{10,1... | collective-permute-start | bytes 786440 | tf_op jit(solution)/shard_map/ppermute | solution.py:14
  (16 other events, 74.0 us)
Sparse Core Ops, SparseCore 0:
  493.5 120.9 all-gather.2
